TPU v7x, 512 devices: a whole 4x8x8 slice. The times are simulated.
512 devices in a mesh: rows: 16 (over z, core), feats: 32 (over x, y).
Axes of the slice: x: 4, y: 8, z: 8, core: 2. Of those that a mesh axis runs over, the one named last changes fastest.
Arguments:
- bin_index: int32 [2048, 32768], P('feats', 'rows'), may hold values from 0 to 255
- gradient: bfloat16 [32768], P('rows'), may hold values from -6 to 6
- hessian: bfloat16 [32768], P('rows'), may hold values from 0.049804688 to 1
- node_id: int32 [32768], P('rows'), may hold values from 0 to 15
- split_feature: int32 [16], replicated, may hold values from 0 to 2047
- split_bin: int32 [16], replicated, may hold values from 0 to 255
Outputs:
- split_gain: float32 [2048, 16, 256], P(('feats', 'rows'))
- best_gain: float32 [16], replicated
- child_id: int32 [32768], P('rows')
All inputs are finite; a program needn't handle non-finite values.
Results may differ from a plain program's by a relative error of at most 0.0003.
Values may be sent and summed in bfloat16 or wider, within the bound.
A program may use at most 64 MiB of HBM per device.

v0:
```python
import math

import jax
import jax.numpy as jnp
from jax import lax
from jax.sharding import PartitionSpec as P

BINS = 256


def bin_histogram(columns, weights, nbins):
    width, row_count = columns.shape
    group = math.gcd(width, 8)
    blocks = columns.reshape(width // group, group, row_count)
    levels = jnp.arange(nbins, dtype=jnp.int32)

    def one_block(block):
        onehot = (block[:, :, None] == levels).astype(jnp.bfloat16)
        return jnp.einsum("grb,rk->gkb", onehot, weights, preferred_element_type=jnp.float32)

    result = lax.map(one_block, blocks)
    return result.reshape(width, weights.shape[1], nbins)


def on_device(bin_index, gradient, hessian, node_id, split_feature, split_bin):
    feat_local, row_count = bin_index.shape
    nodes = split_feature.shape[0]
    node_onehot = (node_id[:, None] == jnp.arange(nodes, dtype=jnp.int32)).astype(jnp.bfloat16)
    weights = jnp.concatenate(
        [node_onehot * gradient[:, None], node_onehot * hessian[:, None]], axis=1
    )
    hist = lax.psum_scatter(
        bin_histogram(bin_index, weights, BINS), "rows", scatter_dimension=0, tiled=True
    )
    grad_hist = hist[:, :nodes]
    hess_hist = hist[:, nodes:]
    left_grad = jnp.cumsum(grad_hist, axis=2)
    left_hess = jnp.cumsum(hess_hist, axis=2)
    total_grad = left_grad[:, :, -1:]
    total_hess = left_hess[:, :, -1:]
    split_gain = (
        left_grad * left_grad / (left_hess + 1.0)
        + (total_grad - left_grad) ** 2 / (total_hess - left_hess + 1.0)
        - total_grad * total_grad / (total_hess + 1.0)
    )
    local_best = jnp.max(split_gain, axis=(0, 2))
    best_gain = lax.pmax(local_best, ("rows", "feats"))
    node_match = node_id[:, None] == jnp.arange(nodes, dtype=jnp.int32)
    feature_of_row = jnp.sum(jnp.where(node_match, split_feature[None, :], 0), axis=1)
    bin_of_row = jnp.sum(jnp.where(node_match, split_bin[None, :], 0), axis=1)
    first_feature = lax.axis_index("feats") * feat_local
    local_column = feature_of_row - first_feature
    mine = (local_column >= 0) & (local_column < feat_local)
    safe_column = jnp.clip(local_column, 0, feat_local - 1)
    chosen = jnp.take_along_axis(bin_index, safe_column[None, :], axis=0)[0]
    right_local = jnp.where(mine & (chosen > bin_of_row), 1, 0).astype(jnp.int32)
    right = lax.psum(right_local, "feats")
    child_id = 2 * node_id + right
    return (split_gain, best_gain, child_id)


def solution(mesh):
    return jax.shard_map(
        on_device,
        mesh=mesh,
        in_specs=(P("feats", "rows"), P("rows"), P("rows"), P("rows"), P(), P()),
        out_specs=(P(("feats", "rows"), None, None), P(), P("rows")),
        check_vma=False,
    )
```

profile of v0, /device:TPU:1, one launch (start us, length us, event | category | flops | bytes accessed | tf_op | source)
XLA Modules:
  0.0 234.1 jit_solution(1627312934535657114)
XLA Ops:
  7.2 0.0 reduce-scatter.2.cloned.1.call-start
  7.2 0.7 fusion.8
  8.0 46.7 %while.11 = (s32[]{:T(128)}, f32[8,8,32,256]{3,2,1,0:T(8,128)}, s32[8,8,2048]{2,1,0:T(8,128)}, bf16[2048,32]{0,1:T(8,128)(2,1)S(1)}, s32[]{:T(128)}) while((s32[]{:T(128)}, f32[8,8,32,256]{3,2,1,0:T(8,128)}, s32[8,8,2048]{2,1,0:T(8,128)}, bf16[2048,32]{0,1:T(8,128)(2,1)S(1)}, s32[]{:T(128)}) %tuple.36), condition=%wide.region_1.2_spmd.clone, body=%wide.region_0.1_spmd.clone.sunk | while | flops 272629760 | bytes 590401 | solution.py:21
  8.0 0.8 dynamic-slice_bitcast_fusion.2
  8.8 5.0 %fusion.22 = f32[8,8,32,256]{3,2,1,0:T(8,128)} fusion(f32[8,8,32,256]{3,2,1,0:T(8,128)} %get-tuple-element.91, s32[]{:T(128)} %get-tuple-element.90, s32[8,2048]{1,0:T(8,128)S(1)} %dynamic-slice_bitcast_fusion.2, bf16[2048,32]{0,1:T(8,128)(2,1)S(1)} %get-tuple-element.98), kind=kOutput, calls=%fused_computation.6.clone.1 | convolution fusion | flops 272629760 | bytes 459264 | tf_op jit(solution)/shard_map/while/body/eval_jaxpr/grb,rk->gkb/dot_general | solution.py:19
  13.8 0.8 dynamic-slice_bitcast_fusion.2
  14.7 5.0 %fusion.22 = f32[8,8,32,256]{3,2,1,0:T(8,128)} fusion(f32[8,8,32,256]{3,2,1,0:T(8,128)} %get-tuple-element.91, s32[]{:T(128)} %get-tuple-element.90, s32[8,2048]{1,0:T(8,128)S(1)} %dynamic-slice_bitcast_fusion.2, bf16[2048,32]{0,1:T(8,128)(2,1)S(1)} %get-tuple-element.98), kind=kOutput, calls=%fused_computation.6.clone.1 | convolution fusion | flops 272629760 | bytes 459264 | tf_op jit(solution)/shard_map/while/body/eval_jaxpr/grb,rk->gkb/dot_general | solution.py:19
  19.7 0.8 dynamic-slice_bitcast_fusion.2
  20.5 5.0 %fusion.22 = f32[8,8,32,256]{3,2,1,0:T(8,128)} fusion(f32[8,8,32,256]{3,2,1,0:T(8,128)} %get-tuple-element.91, s32[]{:T(128)} %get-tuple-element.90, s32[8,2048]{1,0:T(8,128)S(1)} %dynamic-slice_bitcast_fusion.2, bf16[2048,32]{0,1:T(8,128)(2,1)S(1)} %get-tuple-element.98), kind=kOutput, calls=%fused_computation.6.clone.1 | convolution fusion | flops 272629760 | bytes 459264 | tf_op jit(solution)/shard_map/while/body/eval_jaxpr/grb,rk->gkb/dot_general | solution.py:19
  25.5 0.8 dynamic-slice_bitcast_fusion.2
  26.4 5.0 %fusion.22 = f32[8,8,32,256]{3,2,1,0:T(8,128)} fusion(f32[8,8,32,256]{3,2,1,0:T(8,128)} %get-tuple-element.91, s32[]{:T(128)} %get-tuple-element.90, s32[8,2048]{1,0:T(8,128)S(1)} %dynamic-slice_bitcast_fusion.2, bf16[2048,32]{0,1:T(8,128)(2,1)S(1)} %get-tuple-element.98), kind=kOutput, calls=%fused_computation.6.clone.1 | convolution fusion | flops 272629760 | bytes 459264 | tf_op jit(solution)/shard_map/while/body/eval_jaxpr/grb,rk->gkb/dot_general | solution.py:19
  31.3 0.8 dynamic-slice_bitcast_fusion.2
  32.2 5.0 %fusion.22 = f32[8,8,32,256]{3,2,1,0:T(8,128)} fusion(f32[8,8,32,256]{3,2,1,0:T(8,128)} %get-tuple-element.91, s32[]{:T(128)} %get-tuple-element.90, s32[8,2048]{1,0:T(8,128)S(1)} %dynamic-slice_bitcast_fusion.2, bf16[2048,32]{0,1:T(8,128)(2,1)S(1)} %get-tuple-element.98), kind=kOutput, calls=%fused_computation.6.clone.1 | convolution fusion | flops 272629760 | bytes 459264 | tf_op jit(solution)/shard_map/while/body/eval_jaxpr/grb,rk->gkb/dot_general | solution.py:19
  37.2 0.8 dynamic-slice_bitcast_fusion.2
  38.0 5.0 %fusion.22 = f32[8,8,32,256]{3,2,1,0:T(8,128)} fusion(f32[8,8,32,256]{3,2,1,0:T(8,128)} %get-tuple-element.91, s32[]{:T(128)} %get-tuple-element.90, s32[8,2048]{1,0:T(8,128)S(1)} %dynamic-slice_bitcast_fusion.2, bf16[2048,32]{0,1:T(8,128)(2,1)S(1)} %get-tuple-element.98), kind=kOutput, calls=%fused_computation.6.clone.1 | convolution fusion | flops 272629760 | bytes 459264 | tf_op jit(solution)/shard_map/while/body/eval_jaxpr/grb,rk->gkb/dot_general | solution.py:19
  43.0 0.8 dynamic-slice_bitcast_fusion.2
  43.9 5.0 %fusion.22 = f32[8,8,32,256]{3,2,1,0:T(8,128)} fusion(f32[8,8,32,256]{3,2,1,0:T(8,128)} %get-tuple-element.91, s32[]{:T(128)} %get-tuple-element.90, s32[8,2048]{1,0:T(8,128)S(1)} %dynamic-slice_bitcast_fusion.2, bf16[2048,32]{0,1:T(8,128)(2,1)S(1)} %get-tuple-element.98), kind=kOutput, calls=%fused_computation.6.clone.1 | convolution fusion | flops 272629760 | bytes 459264 | tf_op jit(solution)/shard_map/while/body/eval_jaxpr/grb,rk->gkb/dot_general | solution.py:19
  48.8 0.8 dynamic-slice_bitcast_fusion.2
  49.7 5.0 %fusion.22 = f32[8,8,32,256]{3,2,1,0:T(8,128)} fusion(f32[8,8,32,256]{3,2,1,0:T(8,128)} %get-tuple-element.91, s32[]{:T(128)} %get-tuple-element.90, s32[8,2048]{1,0:T(8,128)S(1)} %dynamic-slice_bitcast_fusion.2, bf16[2048,32]{0,1:T(8,128)(2,1)S(1)} %get-tuple-element.98), kind=kOutput, calls=%fused_computation.6.clone.1 | convolution fusion | flops 272629760 | bytes 459264 | tf_op jit(solution)/shard_map/while/body/eval_jaxpr/grb,rk->gkb/dot_general | solution.py:19
  54.7 0.0 copy-start.1
  54.7 0.0 copy-start.2
  54.7 0.0 copy-start.3
  54.7 0.0 copy-start
  54.7 0.0 reduce-scatter.2.cloned.1.call-update
  54.7 0.7 copy-done.1
  55.4 0.0 copy-done.2
  55.4 0.0 copy-done.3
  55.4 0.1 select_reduce_fusion.1
  55.6 0.2 copy-done
  55.8 16.8 %gather_fusion = s32[2048]{0:T(1024)S(1)} fusion(s32[64,2048]{1,0:T(8,128)S(1)} %bitcast.54, s32[2048]{0:T(1024)S(1)} %bitcast.55), kind=kCustom, calls=%fused_computation | custom fusion | bytes 32768 | tf_op jit(solution)/shard_map/jit(take_along_axis)/gather | solution.py:55
  72.6 18.4 %psum.7 = s32[2048]{0:T(1024)S(1)} all-reduce(s32[2048]{0:T(1024)S(1)} %fusion.14), channel_id=1, replica_groups=mesh['rows'=16,'feats'=32] {'feats'}, use_global_device_ids=true, to_apply=%region_11.12 | all-reduce | flops 2048 | bytes 16384 | tf_op jit(solution)/shard_map/psum | solution.py:57
  90.9 0.6 multiply_add_fusion
  91.5 28.9 %reduce-scatter.2.cloned.1.call-done = f32[4,32,256]{2,1,0:T(8,128)} async-done(((f32[64,32,256]{2,1,0:T(8,128)}), f32[4,32,256]{2,1,0:T(8,128)}) %reduce-scatter.2.cloned.1.call-update) | async-done | bytes 131088 | tf_op jit(solution)/shard_map/reduce_scatter | solution.py:32
  120.5 0.9 slice_bitcast_fusion
  121.4 2.3 reduce-window.16
  123.6 0.1 slice.38
  123.7 0.1 copy.18
  123.9 0.1 copy_bitcast_fusion
  124.0 2.3 reduce-window.14
  126.3 0.1 slice.35
  126.3 0.1 copy.14
  126.5 0.1 copy_bitcast_fusion.1
  126.6 0.2 slice_reduce_fusion.1
  126.8 0.2 subtract_reduce_fusion
  127.0 0.8 add_subtract_fusion
  127.8 99.5 %pmax.7 = f32[16]{0:T(128)} all-reduce(f32[16]{0:T(128)S(1)} %subtract_reduce_fusion), channel_id=1, replica_groups=mesh['rows'=16,'feats'=32] {'rows','feats'}, use_global_device_ids=true, to_apply=%region_8.9 | all-reduce | flops 16 | bytes 128 | tf_op jit(solution)/shard_map/pmax | solution.py:47
  (15 shorter events, 0.1 us)
Async XLA Ops:
  7.2 113.3 %reduce-scatter.2.cloned.1.call-start = ((), (), s32[]{:S(2)}) async-start(), calls=%async_computation.1 | async-start | bytes 2228224 | tf_op jit(solution)/shard_map/reduce_scatter | solution.py:32
  54.7 0.7 copy-start.1
  54.7 0.7 copy-start.2
  54.7 0.7 copy-start.3
  54.7 1.1 copy-start
Sparse Core Ops, SparseCore 0:
  54.8 65.5 reduce-scatter.1
where the time goes:
time: 235 us; the launch traced here: 234 us
  blocking collectives  118 us (50%)
  matrix products  39.9 us (17%)
  waiting for transfers between devices  28.9 us (12%)
  local copies, waits for them, and re-layouts  25.7 us (11%)
  between operations  14.2 us (6%)
  other arithmetic  7.53 us (3%)
    pmax x1, blocking collectives, on_device(): best_gain = lax.pmax(local_best, ('rows', 'feats'))  99.5 us
    dot_general x8, matrix products, one_block(): jnp.einsum('grb,rk->gkb', onehot, weights, preferred_element_type=jnp.flo...  39.9 us
    reduce_scatter x1, waiting for transfers between devices, on_device(): lax.psum_scatter(bin_histogram(bin_index, weights, BINS), 'rows', scatter...  28.9 us
    psum x1, blocking collectives, on_device(): right = lax.psum(right_local, 'feats')  18.4 us
    gather x1, local copies, waits for them, and re-layouts, on_device(): chosen = jnp.take_along_axis(bin_index, safe_column[None, :], axis=0)[0]  16.8 us
    eq x8, local copies, waits for them, and re-layouts, one_block(): onehot = (block[:, :, None] == levels).astype(jnp.bfloat16)  6.75 us
    another operation x6, other arithmetic  4.77 us
  transfers between devices with their start and end apart: 1, of which 1 were waited for; matrix products, arithmetic and copies ran while one was open for 8% of the time, Pallas kernels for 0%

commit v1 on v0

v1 whole, which is shorter than its diff:
```python
import functools

import jax
import jax.numpy as jnp
from jax import lax
from jax.experimental import pallas as pl
from jax.experimental.pallas import tpu as pltpu
from jax.sharding import PartitionSpec as P

BINS = 256
LO = 64
HI = BINS // LO
NODES = 16
LANES = 128
BF16 = jnp.bfloat16
MESH = pl.DeviceIdType.MESH


def sublane_index(rows, lanes):
    return lax.broadcasted_iota(jnp.int32, (rows, lanes), 0)


def as_bf16(x):
    return x.astype(jnp.float32).astype(BF16)


def kernel(R, F, own, sf_ref, sb_ref, bins_ref, grad_ref, hess_ref, node_ref, node_row_ref,
           gain_ref, best_ref, child_ref,
           bins_v, picked, send, recv, acc, right, rights, top, tops, high, highs,
           in_sem, send_sem, recv_sem, rsend_sem, rrecv_sem, tsend_sem, trecv_sem, hsend_sem, hrecv_sem):
    feat_local, row_count = bins_v.shape
    tiles = row_count // LANES
    me_r = lax.axis_index("rows")
    me_f = lax.axis_index("feats")

    load = pltpu.make_async_copy(bins_ref, bins_v, in_sem)
    load.start()

    barrier = pltpu.get_barrier_semaphore()

    def greet_rows(k, c):
        pl.semaphore_signal(barrier, inc=1, device_id=(lax.rem(me_r + k, R), me_f), device_id_type=MESH)
        return c

    def greet_feats(k, c):
        pl.semaphore_signal(barrier, inc=1, device_id=(me_r, lax.rem(me_f + k, F)), device_id_type=MESH)
        return c

    lax.fori_loop(1, R, greet_rows, 0)
    lax.fori_loop(1, F, greet_feats, 0)

    grad = grad_ref[...]
    hess = hess_ref[...]
    node = node_ref[...]
    node16 = as_bf16(node)
    load.wait()
    for j in range(R):
        block = bins_v[j * own:(j + 1) * own, :]
        stacked = jnp.concatenate([block[:, t * LANES:(t + 1) * LANES] for t in range(tiles)], axis=0)
        send[j, 0:own * tiles, :] = as_bf16(stacked)
        send[j, own * tiles:(own + 1) * tiles, :] = grad
        send[j, (own + 1) * tiles:(own + 2) * tiles, :] = hess
        send[j, (own + 2) * tiles:(own + 3) * tiles, :] = node16
    recv[0] = send[me_r]

    pl.semaphore_wait(barrier, R + F - 2)

    def offset(i):
        odd = lax.rem(i, 2)
        return odd * ((i + 1) // 2) + (1 - odd) * lax.rem(R - i // 2, R)

    def chunk_copy(k):
        to = lax.rem(me_r + k, R)
        return pltpu.make_async_remote_copy(
            src_ref=send.at[to], dst_ref=recv.at[k], send_sem=send_sem.at[k], recv_sem=recv_sem.at[k],
            device_id=(to, me_f), device_id_type=MESH)

    def right_copy(k):
        return pltpu.make_async_remote_copy(
            src_ref=right, dst_ref=rights.at[k], send_sem=rsend_sem.at[k], recv_sem=rrecv_sem.at[k],
            device_id=(me_r, lax.rem(me_f + k, F)), device_id_type=MESH)

    def top_copy(k):
        return pltpu.make_async_remote_copy(
            src_ref=top, dst_ref=tops.at[k], send_sem=tsend_sem.at[k], recv_sem=trecv_sem.at[k],
            device_id=(lax.rem(me_r + k, R), me_f), device_id_type=MESH)

    def high_copy(k):
        return pltpu.make_async_remote_copy(
            src_ref=high, dst_ref=highs.at[k], send_sem=hsend_sem.at[k], recv_sem=hrecv_sem.at[k],
            device_id=(me_r, lax.rem(me_f + k, F)), device_id_type=MESH)

    def start(copy, k, c):
        copy(k).start()
        return c

    def wait_recv(copy, k, c):
        copy(k).wait_recv()
        return c

    def wait_send(copy, k, c):
        copy(k).wait_send()
        return c

    lax.fori_loop(1, R, lambda i, c: start(chunk_copy, offset(i), c), 0)

    first = me_f * feat_local
    split = jnp.zeros((NODES, LANES), jnp.int32)
    mine = jnp.zeros((NODES, LANES), jnp.int32)
    index = sublane_index(NODES, LANES)
    for n in range(NODES):
        column = sf_ref[n] - first
        held = jnp.where(column >= 0, 1, 0) * jnp.where(column < feat_local, 1, 0)
        picked[n:n + 1, :] = bins_v[pl.ds(jnp.clip(column, 0, feat_local - 1), 1), :]
        split = jnp.where(index == n, sb_ref[n], split)
        mine = jnp.where(index == n, held, mine)
    node_row = node_row_ref[...]
    parts = []
    for t in range(tiles):
        lanes = slice(t * LANES, (t + 1) * LANES)
        goes = jnp.where(picked[:, lanes] > split, mine, 0)
        goes = jnp.where(jnp.broadcast_to(node_row[:, lanes], (NODES, LANES)) == index, goes, 0)
        parts.append(jnp.sum(goes.astype(jnp.float32), axis=0, keepdims=True))
    right[...] = jnp.concatenate(parts, axis=0).astype(BF16)
    lax.fori_loop(1, F, lambda k, c: start(right_copy, k, c), 0)

    acc[...] = jnp.zeros_like(acc)
    span = 4
    depth = span * LANES
    zero = jnp.zeros((NODES, depth), BF16)

    def over_lanes(slot, base, q, stride, rows):
        return jnp.concatenate(
            [jnp.broadcast_to(recv[slot, pl.ds(base + (q * span + s) * stride, 1), :], (rows, LANES))
             for s in range(span)], axis=1)

    def add_chunk(slot):
        for q in range(tiles // span):
            here = over_lanes(slot, (own + 2) * tiles, q, 1, NODES) == as_bf16(sublane_index(NODES, depth))
            wg = jnp.where(here, over_lanes(slot, own * tiles, q, 1, NODES), zero)
            wh = jnp.where(here, over_lanes(slot, (own + 1) * tiles, q, 1, NODES), zero)
            levels = as_bf16(sublane_index(LO, depth))
            for f in range(own):
                b = over_lanes(slot, f, q, own, 1).astype(jnp.float32)
                hi = jnp.floor(b * (1.0 / LO))
                lo = (b - hi * LO).astype(BF16)
                hi = jnp.broadcast_to(hi.astype(BF16), (NODES, depth))
                sides = []
                for level in range(HI):
                    at = hi == BF16(level)
                    sides += [jnp.where(at, wg, zero), jnp.where(at, wh, zero)]
                moving = jnp.concatenate(sides, axis=0)
                steps = jnp.where(jnp.broadcast_to(lo, (LO, depth)) <= levels, BF16(1), BF16(0))
                acc[f] += lax.dot_general(
                    moving, steps, (((1,), (1,)), ((), ())), preferred_element_type=jnp.float32)

    add_chunk(0)

    def one_source(i, c):
        k = offset(i)
        chunk_copy(k).wait_recv()
        add_chunk(k)
        return c

    lax.fori_loop(1, R, one_source, 0)

    best = jnp.full((NODES, 1), -jnp.inf, jnp.float32)
    for f in range(own):
        blocks = []
        carry = jnp.zeros((2 * NODES, 1), jnp.float32)
        for level in range(HI):
            block = acc[f, level * 2 * NODES:(level + 1) * 2 * NODES, :] + carry
            carry = block[:, LO - 1:LO]
            blocks.append(block)
        left = jnp.concatenate(blocks, axis=1)
        left_grad, left_hess = left[:NODES], left[NODES:]
        total_grad, total_hess = carry[:NODES], carry[NODES:]
        right_grad = total_grad - left_grad
        gain = (left_grad * left_grad / (left_hess + 1.0)
                + right_grad * right_grad / (total_hess - left_hess + 1.0)
                - total_grad * total_grad / (total_hess + 1.0))
        gain_ref[f] = gain
        best = jnp.maximum(best, jnp.max(gain, axis=1, keepdims=True))

    diagonal = index == lax.broadcasted_iota(jnp.int32, (NODES, LANES), 1)
    top[...] = jnp.max(jnp.where(diagonal, best, -jnp.inf), axis=0, keepdims=True)
    tops[0] = top[...]
    lax.fori_loop(1, R, lambda k, c: start(top_copy, k, c), 0)

    rights[0] = right[...]
    lax.fori_loop(1, F, lambda k, c: wait_recv(right_copy, k, c), 0)
    goes_right = jnp.zeros((tiles, LANES), jnp.float32)
    for k in range(F):
        goes_right = goes_right + rights[k].astype(jnp.float32)
    child_ref[...] = 2 * node + goes_right.astype(jnp.int32)

    lax.fori_loop(1, R, lambda k, c: wait_recv(top_copy, k, c), 0)
    high[...] = jnp.max(tops[...], axis=0)
    highs[0] = high[...]
    lax.fori_loop(1, F, lambda k, c: start(high_copy, k, c), 0)
    lax.fori_loop(1, R, lambda k, c: wait_send(chunk_copy, k, c), 0)
    lax.fori_loop(1, F, lambda k, c: wait_send(right_copy, k, c), 0)
    lax.fori_loop(1, R, lambda k, c: wait_send(top_copy, k, c), 0)
    lax.fori_loop(1, F, lambda k, c: wait_recv(high_copy, k, c), 0)
    best_ref[...] = jnp.max(highs[...], axis=0)
    lax.fori_loop(1, F, lambda k, c: wait_send(high_copy, k, c), 0)


def on_device(R, F, bin_index, gradient, hessian, node_id, split_feature, split_bin):
    feat_local, row_count = bin_index.shape
    own = feat_local // R
    tiles = row_count // LANES
    rows = (own + 3) * tiles
    vmem = pl.BlockSpec(memory_space=pltpu.VMEM)
    smem = pl.BlockSpec(memory_space=pltpu.SMEM)
    dma = pltpu.SemaphoreType.DMA
    gain, best, child = pl.pallas_call(
        functools.partial(kernel, R, F, own),
        out_shape=(
            jax.ShapeDtypeStruct((own, NODES, BINS), jnp.float32),
            jax.ShapeDtypeStruct((1, LANES), jnp.float32),
            jax.ShapeDtypeStruct((tiles, LANES), jnp.int32),
        ),
        in_specs=[smem, smem, pl.BlockSpec(memory_space=pl.ANY), vmem, vmem, vmem, vmem],
        out_specs=(vmem, vmem, vmem),
        scratch_shapes=[
            pltpu.VMEM((feat_local, row_count), jnp.int32),
            pltpu.VMEM((NODES, row_count), jnp.int32),
            pltpu.VMEM((R, rows, LANES), BF16),
            pltpu.VMEM((R, rows, LANES), BF16),
            pltpu.VMEM((own, 2 * NODES * HI, LO), jnp.float32),
            pltpu.VMEM((tiles, LANES), BF16),
            pltpu.VMEM((F, tiles, LANES), BF16),
            pltpu.VMEM((1, LANES), jnp.float32),
            pltpu.VMEM((R, 1, LANES), jnp.float32),
            pltpu.VMEM((1, LANES), jnp.float32),
            pltpu.VMEM((F, 1, LANES), jnp.float32),
            dma(()),
            dma((R,)), dma((R,)),
            dma((F,)), dma((F,)),
            dma((R,)), dma((R,)),
            dma((F,)), dma((F,)),
        ],
        compiler_params=pltpu.CompilerParams(
            collective_id=0, has_side_effects=True, vmem_limit_bytes=32 << 20),
    )(
        split_feature, split_bin, bin_index,
        gradient.reshape(tiles, LANES), hessian.reshape(tiles, LANES),
        node_id.reshape(tiles, LANES), node_id.reshape(1, row_count),
    )
    return gain, best[0, :NODES], child.reshape(row_count)


def solution(mesh):
    return jax.shard_map(
        functools.partial(on_device, mesh.shape["rows"], mesh.shape["feats"]),
        mesh=mesh,
        in_specs=(P("feats", "rows"), P("rows"), P("rows"), P("rows"), P(), P()),
        out_specs=(P(("feats", "rows"), None, None), P(), P("rows")),
        check_vma=False,
    )
```

time: 235 us -> 49.3 us (0.21)
  blocking collectives: 118 us -> 0 us
  Pallas kernels: 0 us -> 43.5 us
  matrix products: 39.9 us -> 0 us
  waiting for transfers between devices: 28.9 us -> 0 us
  local copies, waits for them, and re-layouts: 25.7 us -> 4.83 us
  between operations: 14.2 us -> 0.67 us
  other arithmetic: 7.53 us -> 0 us
    pmax x1 -> x0, blocking collectives: 99.5 us -> none  [on_device(): best_gain = lax.pmax(local_best, ('rows', 'feats'))]
    pallas_call x0 -> x1, Pallas kernels: none -> 43.5 us  [on_device(): pl.pallas_call(functools.partial(kernel, R, F, own), out_shape=(jax.Shape...]
    dot_general x8 -> x0, matrix products: 39.9 us -> none  [one_block(): jnp.einsum('grb,rk->gkb', onehot, weights, preferred_element_type=jnp.flo...]
    reduce_scatter x1 -> x0, waiting for transfers between devices: 28.9 us -> none  [on_device(): lax.psum_scatter(bin_histogram(bin_index, weights, BINS), 'rows', scatter...]
    psum x1 -> x0, blocking collectives: 18.4 us -> none  [on_device(): right = lax.psum(right_local, 'feats')]
    gather x1 -> x0, local copies, waits for them, and re-layouts: 16.8 us -> none  [on_device(): chosen = jnp.take_along_axis(bin_index, safe_column[None, :], axis=0)[0]]
    eq x8 -> x0, local copies, waits for them, and re-layouts: 6.75 us -> none  [one_block(): onehot = (block[:, :, None] == levels).astype(jnp.bfloat16)]
    another operation x6 -> x0, other arithmetic: 4.77 us -> none
  transfers between devices with their start and end apart: 1 -> 0, of which waited for: 1 -> 0; matrix products, arithmetic and copies ran while one was open for 8% -> 0% of each run, Pallas kernels for 0% -> 0%
where the time goes in v1:
time: 49.3 us; the launch traced here: 49 us
  Pallas kernels  43.5 us (88%)
  local copies, waits for them, and re-layouts  4.83 us (10%)
  between operations  0.67 us (1%)
    pallas_call x1, Pallas kernels, on_device(): pl.pallas_call(functools.partial(kernel, R, F, own), out_shape=(jax.Shape...  43.5 us
    unnamed x14, local copies, waits for them, and re-layouts  4.32 us

profile of v1, /device:TPU:1, one launch (start us, length us, event | category | flops | bytes accessed | tf_op | source)
XLA Modules:
  0.0 49.0 jit_solution(11021316088535598196)
XLA Ops:
  0.6 0.0 copy-start.2
  0.6 0.0 copy-start.4
  0.7 0.0 copy-start.5
  0.7 0.7 %copy-done.2 = bf16[2048]{0:T(1024)(128)(2,1)S(1)} copy-done((bf16[2048]{0:T(1024)(128)(2,1)S(1)}, bf16[2048]{0:T(1024)(128)(2,1)}, u32[]{:S(2)}) %copy-start.2) | copy-done | bytes 4120
  1.3 0.0 copy-done.4
  1.3 0.0 copy-done.5
  1.3 0.0 copy-start
  1.3 1.0 %copy-done = s32[64,2048]{1,0:T(8,128)S(1)} copy-done((s32[64,2048]{1,0:T(8,128)S(1)}, s32[64,2048]{1,0:T(8,128)}, u32[]{:S(2)}) %copy-start) | copy-done | bytes 524312
  2.4 0.0 copy-start.1
  2.4 0.7 %copy-done.1 = s32[2048]{0:T(1024)S(1)} copy-done((s32[2048]{0:T(1024)S(1)}, s32[2048]{0:T(1024)}, u32[]{:S(2)}) %copy-start.1) | copy-done | bytes 8216
  3.1 0.0 copy-start.3
  3.1 0.7 %copy-done.3 = bf16[2048]{0:T(1024)(128)(2,1)S(1)} copy-done((bf16[2048]{0:T(1024)(128)(2,1)S(1)}, bf16[2048]{0:T(1024)(128)(2,1)}, u32[]{:S(2)}) %copy-start.3) | copy-done | bytes 4120
  3.8 43.5 %shard_map.85 = (f32[4,16,256]{2,1,0:T(8,128)S(1)}, f32[1,128]{1,0:T(1,128)S(1)}, s32[16,128]{1,0:T(8,128)S(1)}) custom-call(s32[16]{0:T(128)S(1)} %copy-done.4, s32[16]{0:T(128)S(1)} %copy-done.5, s32[64,2048]{1,0:T(8,128)S(1)} %copy-done, bf16[16,128]{1,0:T(8,128)(2,1)S(1)} %bitcast.10, bf16[16,128]{1,0:T(8,128)(2,1)S(1)} %bitcast.11, ...), custom_call_target="tpu_custom_call" | custom-call | tf_op jit(solution)/shard_map/pallas_call | solution.py:217
  47.3 0.5 %slice_bitcast_fusion = f32[16]{0:T(128)} fusion(f32[1,128]{1,0:T(1,128)S(1)} %get-tuple-element.7), kind=kLoop, calls=%fused_computation | loop fusion | bytes 128 | tf_op jit(solution)/shard_map/squeeze | solution.py:251
  47.8 0.6 %copy.11 = f32[4,16,256]{2,1,0:T(8,128)} copy(f32[4,16,256]{2,1,0:T(8,128)S(1)} %get-tuple-element.12) | data formatting | bytes 131072
  48.4 0.6 %copy.12 = s32[2048]{0:T(1024)} copy(s32[2048]{0:T(1024)S(1)} %bitcast.9) | data formatting | bytes 16384
Async XLA Ops:
  0.6 0.7 %copy-start.2 = (bf16[2048]{0:T(1024)(128)(2,1)S(1)}, bf16[2048]{0:T(1024)(128)(2,1)}, u32[]{:S(2)}) copy-start(bf16[2048]{0:T(1024)(128)(2,1)} %param.7) | copy-start | bytes 12292
  0.6 0.7 %copy-start.4 = (s32[16]{0:T(128)S(1)}, s32[16]{0:T(128)}, u32[]{:S(2)}) copy-start(s32[16]{0:T(128)} %sf_ref.1) | copy-start | bytes 196
  0.7 0.7 %copy-start.5 = (s32[16]{0:T(128)S(1)}, s32[16]{0:T(128)}, u32[]{:S(2)}) copy-start(s32[16]{0:T(128)} %sb_ref.1) | copy-start | bytes 196
  1.3 1.0 %copy-start = (s32[64,2048]{1,0:T(8,128)S(1)}, s32[64,2048]{1,0:T(8,128)}, u32[]{:S(2)}) copy-start(s32[64,2048]{1,0:T(8,128)} %bins_ref.1) | copy-start | bytes 1572868
  2.4 0.7 %copy-start.1 = (s32[2048]{0:T(1024)S(1)}, s32[2048]{0:T(1024)}, u32[]{:S(2)}) copy-start(s32[2048]{0:T(1024)} %param.9) | copy-start | bytes 24580
  3.1 0.7 %copy-start.3 = (bf16[2048]{0:T(1024)(128)(2,1)S(1)}, bf16[2048]{0:T(1024)(128)(2,1)}, u32[]{:S(2)}) copy-start(bf16[2048]{0:T(1024)(128)(2,1)} %param.8) | copy-start | bytes 12292

commit v2 on v1

v2 whole, which is shorter than its diff:
```python
import functools

import jax
import jax.numpy as jnp
from jax import lax
from jax.experimental import pallas as pl
from jax.experimental.pallas import tpu as pltpu
from jax.sharding import PartitionSpec as P

BINS = 256
LO = 64
HI = BINS // LO
NODES = 16
LANES = 128
BF16 = jnp.bfloat16
MESH = pl.DeviceIdType.MESH
FIRST = 3


def sublane_index(rows, lanes):
    return lax.broadcasted_iota(jnp.int32, (rows, lanes), 0)


def as_bf16(x):
    return x.astype(jnp.float32).astype(BF16)


def kernel(R, F, own, sf_ref, sb_ref, bins_ref, grad_ref, hess_ref, node_ref, node_row_ref,
           gain_ref, best_ref, child_ref,
           bins_v, picked, node_v, node_row_v, send, recv, weights, acc, right, rights, top, tops, high, highs,
           in_sem, send_sem, recv_sem, wsend_sem, wrecv_sem, fsend_sem, frecv_sem,
           rsend_sem, rrecv_sem, tsend_sem, trecv_sem, hsend_sem, hrecv_sem):
    feat_local, row_count = bins_v.shape
    tiles = row_count // LANES
    Z = R // 2
    me_r = lax.axis_index("rows")
    me_f = lax.axis_index("feats")
    me_z = me_r // 2
    core = lax.rem(me_r, 2)

    loads = [
        pltpu.make_async_copy(bins_ref, bins_v, in_sem.at[0]),
        pltpu.make_async_copy(grad_ref, weights.at[0, 0, 0:tiles, :], in_sem.at[1]),
        pltpu.make_async_copy(hess_ref, weights.at[0, 0, tiles:2 * tiles, :], in_sem.at[2]),
        pltpu.make_async_copy(node_ref, node_v, in_sem.at[3]),
        pltpu.make_async_copy(node_row_ref, node_row_v, in_sem.at[4]),
    ]
    for load in loads:
        load.start()

    barrier = pltpu.get_barrier_semaphore()

    def greet_rows(k, c):
        pl.semaphore_signal(barrier, inc=1, device_id=(lax.rem(me_r + k, R), me_f), device_id_type=MESH)
        return c

    def greet_feats(k, c):
        pl.semaphore_signal(barrier, inc=1, device_id=(me_r, lax.rem(me_f + k, F)), device_id_type=MESH)
        return c

    lax.fori_loop(F // 2, F, greet_feats, 0)
    lax.fori_loop(1, F // 2, greet_feats, 0)
    lax.fori_loop(1, R, greet_rows, 0)

    for load in loads:
        load.wait()
    weights[0, 0, 2 * tiles:3 * tiles, :] = as_bf16(node_v[...])
    for j in range(R):
        block = bins_v[j * own:(j + 1) * own, :]
        send[j] = as_bf16(jnp.concatenate([block[:, t * LANES:(t + 1) * LANES] for t in range(tiles)], axis=0))
    recv[0, 0] = send[me_r]

    pl.semaphore_wait(barrier, R + F - 2)

    def bins_copy(d, o):
        to = 2 * lax.rem(me_z + d, Z) + (core if o == 0 else 1 - core)
        return bins_copy_to(d, o, to)

    def bins_copy_from(d, o):
        return bins_copy_to(d, o, 2 * me_z + 1 - core)

    def bins_copy_to(d, o, to):
        return pltpu.make_async_remote_copy(
            src_ref=send.at[to], dst_ref=recv.at[d, o], send_sem=send_sem.at[d, o], recv_sem=recv_sem.at[d, o],
            device_id=(to, me_f), device_id_type=MESH)

    def weights_copy(d):
        return pltpu.make_async_remote_copy(
            src_ref=weights.at[0, 0], dst_ref=weights.at[d, 0], send_sem=wsend_sem.at[d], recv_sem=wrecv_sem.at[d],
            device_id=(2 * lax.rem(me_z + d, Z) + core, me_f), device_id_type=MESH)

    def forward_copy(d):
        return pltpu.make_async_remote_copy(
            src_ref=weights.at[d, 0], dst_ref=weights.at[d, 1], send_sem=fsend_sem.at[d], recv_sem=frecv_sem.at[d],
            device_id=(2 * me_z + 1 - core, me_f), device_id_type=MESH)

    def right_copy(k):
        return pltpu.make_async_remote_copy(
            src_ref=right, dst_ref=rights.at[k], send_sem=rsend_sem.at[k], recv_sem=rrecv_sem.at[k],
            device_id=(me_r, lax.rem(me_f + k, F)), device_id_type=MESH)

    def top_copy(k):
        return pltpu.make_async_remote_copy(
            src_ref=top, dst_ref=tops.at[k], send_sem=tsend_sem.at[k], recv_sem=trecv_sem.at[k],
            device_id=(lax.rem(me_r + k, R), me_f), device_id_type=MESH)

    def high_copy(k):
        return pltpu.make_async_remote_copy(
            src_ref=high, dst_ref=highs.at[k], send_sem=hsend_sem.at[k], recv_sem=hrecv_sem.at[k],
            device_id=(me_r, lax.rem(me_f + k, F)), device_id_type=MESH)

    def start(copy, k, c):
        copy(k).start()
        return c

    def wait_recv(copy, k, c):
        copy(k).wait_recv()
        return c

    def wait_send(copy, k, c):
        copy(k).wait_send()
        return c

    def distance(i):
        odd = lax.rem(i, 2)
        return odd * ((i + 1) // 2) + (1 - odd) * (Z - i // 2)

    forward_copy(0).start()
    bins_copy(0, 1).start()
    weights_copy(distance(1)).start()

    def send_round(i):
        @pl.when(i < Z - 1)
        def _():
            weights_copy(distance(i + 1)).start()

        bins_copy(distance(i), 0).start()
        bins_copy(distance(i), 1).start()

    def first_round(i, c):
        send_round(i)
        return c

    lax.fori_loop(1, FIRST + 1, first_round, 0)

    span = 2
    depth = span * LANES
    blocks_of_chunk = tiles // span
    zero = jnp.zeros((NODES, depth), BF16)
    high_rows = 2 * NODES * HI

    def over_lanes(ref, d, o, base, t, stride, rows):
        return jnp.concatenate(
            [jnp.broadcast_to(ref[d, o, pl.ds(base + (t * span + s) * stride, 1), :], (rows, LANES))
             for s in range(span)], axis=1)

    def push(chunk, t):
        d, o = chunk
        levels = as_bf16(sublane_index(LO, depth))
        steps = []
        for f in range(own):
            b = over_lanes(recv, d, o, f, t, own, 1).astype(jnp.float32)
            low = (b - jnp.floor(b * (1.0 / LO)) * LO).astype(BF16)
            steps.append(jnp.where(jnp.broadcast_to(low, (LO, depth)) <= levels, BF16(1), BF16(0)))
        pltpu.matmul_push_rhs(jnp.concatenate(steps, axis=0), (t // 2) % 2, t % 2, transpose=True)

    def stream(accs, chunk, t):
        d, o = chunk
        here = over_lanes(weights, d, o, 2 * tiles, t, 1, NODES) == as_bf16(sublane_index(NODES, depth))
        wg = jnp.where(here, over_lanes(weights, d, o, 0, t, 1, NODES), zero)
        wh = jnp.where(here, over_lanes(weights, d, o, tiles, t, 1, NODES), zero)
        sides = []
        for f in range(own):
            b = over_lanes(recv, d, o, f, t, own, 1).astype(jnp.float32)
            part = jnp.broadcast_to(jnp.floor(b * (1.0 / LO)).astype(BF16), (NODES, depth))
            for level in range(HI):
                at = part == BF16(level)
                sides += [jnp.where(at, wg, zero), jnp.where(at, wh, zero)]
        pltpu.matmul_acc_lhs(accs[t % 2], jnp.concatenate(sides, axis=0), (t // 2) % 2)

    def pass_on(d):
        weights_copy(d).wait_recv()
        forward_copy(d).start()

    def chunk_of(k):
        i = k // 2
        return jnp.where(i == 0, 0, distance(i)), lax.rem(k, 2)

    def await_chunk(k):
        d, o = chunk_of(k)
        bins_copy_from(d, o).wait_recv()

        @pl.when(o == 1)
        def _():
            forward_copy(d).wait_recv()

        return d, o

    def accumulate(*accs):
        push((0, 0), 0)
        push((0, 0), 1)

        def one_chunk(k, c):
            chunk = chunk_of(k)

            @pl.when((lax.rem(k, 2) == 1) & (k < R - 1))
            def _():
                pass_on(distance(k // 2 + 1))

            @pl.when((lax.rem(k, 2) == 0) & (k // 2 + FIRST + 1 < Z))
            def _():
                send_round(k // 2 + FIRST + 1)

            for t in range(blocks_of_chunk - 2):
                stream(accs, chunk, t)
                push(chunk, t + 2)
            following = await_chunk(k + 1)
            for t in range(blocks_of_chunk - 2, blocks_of_chunk):
                stream(accs, chunk, t)
                push(following, t + 2 - blocks_of_chunk)
            return c

        lax.fori_loop(0, R - 1, one_chunk, 0)
        chunk = chunk_of(R - 1)
        for t in range(blocks_of_chunk):
            stream(accs, chunk, t)
            if t + 2 < blocks_of_chunk:
                push(chunk, t + 2)
        total = pltpu.matmul_pop(accs[0]) + pltpu.matmul_pop(accs[1])
        for f in range(own):
            acc[f] = total[f * high_rows:(f + 1) * high_rows, f * LO:(f + 1) * LO]

    with jax.sharding.use_abstract_mesh(jax.sharding.get_abstract_mesh()):
        pl.run_scoped(
            accumulate,
            pltpu.ACC(0)((own * high_rows, own * LO), jnp.float32),
            pltpu.ACC(1)((own * high_rows, own * LO), jnp.float32))

    best = jnp.full((NODES, 1), -jnp.inf, jnp.float32)
    for f in range(own):
        blocks = []
        carry = jnp.zeros((2 * NODES, 1), jnp.float32)
        for level in range(HI):
            block = acc[f, level * 2 * NODES:(level + 1) * 2 * NODES, :] + carry
            carry = block[:, LO - 1:LO]
            blocks.append(block)
        left = jnp.concatenate(blocks, axis=1)
        left_grad, left_hess = left[:NODES], left[NODES:]
        total_grad, total_hess = carry[:NODES], carry[NODES:]
        right_grad = total_grad - left_grad
        gain = (left_grad * left_grad / (left_hess + 1.0)
                + right_grad * right_grad / (total_hess - left_hess + 1.0)
                - total_grad * total_grad / (total_hess + 1.0))
        gain_ref[f] = gain
        best = jnp.maximum(best, jnp.max(gain, axis=1, keepdims=True))

    index = sublane_index(NODES, LANES)
    diagonal = index == lax.broadcasted_iota(jnp.int32, (NODES, LANES), 1)
    top[...] = jnp.max(jnp.where(diagonal, best, -jnp.inf), axis=0, keepdims=True)
    tops[0] = top[...]
    lax.fori_loop(1, R, lambda k, c: start(top_copy, k, c), 0)

    first = me_f * feat_local
    split = jnp.zeros((NODES, LANES), jnp.int32)
    mine = jnp.zeros((NODES, LANES), jnp.int32)
    for n in range(NODES):
        column = sf_ref[n] - first
        held = jnp.where(column >= 0, 1, 0) * jnp.where(column < feat_local, 1, 0)
        picked[n:n + 1, :] = bins_v[pl.ds(jnp.clip(column, 0, feat_local - 1), 1), :]
        split = jnp.where(index == n, sb_ref[n], split)
        mine = jnp.where(index == n, held, mine)
    node_row = node_row_v[...]
    parts = []
    for t in range(tiles):
        lanes = slice(t * LANES, (t + 1) * LANES)
        goes = jnp.where(picked[:, lanes] > split, mine, 0)
        goes = jnp.where(jnp.broadcast_to(node_row[:, lanes], (NODES, LANES)) == index, goes, 0)
        parts.append(jnp.sum(goes.astype(jnp.float32), axis=0, keepdims=True))
    right[...] = jnp.concatenate(parts, axis=0).astype(BF16)
    lax.fori_loop(1, F, lambda k, c: start(right_copy, k, c), 0)

    lax.fori_loop(1, R, lambda k, c: wait_recv(top_copy, k, c), 0)
    high[...] = jnp.max(tops[...], axis=0)
    highs[0] = high[...]
    lax.fori_loop(1, F, lambda k, c: start(high_copy, k, c), 0)

    rights[0] = right[...]
    lax.fori_loop(1, F, lambda k, c: wait_recv(right_copy, k, c), 0)
    goes_right = jnp.zeros((tiles, LANES), jnp.float32)
    for k in range(F):
        goes_right = goes_right + rights[k].astype(jnp.float32)
    child_ref[...] = 2 * node_v[...] + goes_right.astype(jnp.int32)

    def sent(d, c):
        weights_copy(d).wait_send()
        bins_copy(d, 0).wait_send()
        bins_copy(d, 1).wait_send()
        forward_copy(d).wait_send()
        return c

    forward_copy(0).wait_send()
    bins_copy(0, 1).wait_send()
    lax.fori_loop(1, Z, sent, 0)
    lax.fori_loop(1, F, lambda k, c: wait_send(right_copy, k, c), 0)
    lax.fori_loop(1, R, lambda k, c: wait_send(top_copy, k, c), 0)
    lax.fori_loop(1, F, lambda k, c: wait_recv(high_copy, k, c), 0)
    best_ref[...] = jnp.max(highs[...], axis=0)
    lax.fori_loop(1, F, lambda k, c: wait_send(high_copy, k, c), 0)


def on_device(R, F, bin_index, gradient, hessian, node_id, split_feature, split_bin):
    feat_local, row_count = bin_index.shape
    own = feat_local // R
    tiles = row_count // LANES
    vmem = pl.BlockSpec(memory_space=pltpu.VMEM)
    smem = pl.BlockSpec(memory_space=pltpu.SMEM)
    hbm = pl.BlockSpec(memory_space=pltpu.HBM)
    dma = pltpu.SemaphoreType.DMA
    gain, best, child = pl.pallas_call(
        functools.partial(kernel, R, F, own),
        out_shape=(
            jax.ShapeDtypeStruct((own, NODES, BINS), jnp.float32),
            jax.ShapeDtypeStruct((1, LANES), jnp.float32),
            jax.ShapeDtypeStruct((tiles, LANES), jnp.int32),
        ),
        in_specs=[smem, smem, hbm, hbm, hbm, hbm, hbm],
        out_specs=(vmem, vmem, vmem),
        scratch_shapes=[
            pltpu.VMEM((feat_local, row_count), jnp.int32),
            pltpu.VMEM((NODES, row_count), jnp.int32),
            pltpu.VMEM((tiles, LANES), jnp.int32),
            pltpu.VMEM((1, row_count), jnp.int32),
            pltpu.VMEM((R, own * tiles, LANES), BF16),
            pltpu.VMEM((R // 2, 2, own * tiles, LANES), BF16),
            pltpu.VMEM((R // 2, 2, 3 * tiles, LANES), BF16),
            pltpu.VMEM((own, 2 * NODES * HI, LO), jnp.float32),
            pltpu.VMEM((tiles, LANES), BF16),
            pltpu.VMEM((F, tiles, LANES), BF16),
            pltpu.VMEM((1, LANES), jnp.float32),
            pltpu.VMEM((R, 1, LANES), jnp.float32),
            pltpu.VMEM((1, LANES), jnp.float32),
            pltpu.VMEM((F, 1, LANES), jnp.float32),
            dma((5,)),
            dma((R // 2, 2)), dma((R // 2, 2)),
            dma((R // 2,)), dma((R // 2,)),
            dma((R // 2,)), dma((R // 2,)),
            dma((F,)), dma((F,)),
            dma((R,)), dma((R,)),
            dma((F,)), dma((F,)),
        ],
        compiler_params=pltpu.CompilerParams(
            collective_id=0, has_side_effects=True, vmem_limit_bytes=60 << 20),
    )(
        split_feature, split_bin, bin_index,
        gradient.reshape(tiles, LANES), hessian.reshape(tiles, LANES),
        node_id.reshape(tiles, LANES), node_id.reshape(1, row_count),
    )
    return gain, best[0, :NODES], child.reshape(row_count)


def solution(mesh):
    return jax.shard_map(
        functools.partial(on_device, mesh.shape["rows"], mesh.shape["feats"]),
        mesh=mesh,
        in_specs=(P("feats", "rows"), P("rows"), P("rows"), P("rows"), P(), P()),
        out_specs=(P(("feats", "rows"), None, None), P(), P("rows")),
        check_vma=False,
    )
```

time: 49.3 us -> 47.9 us (0.972)
  local copies, waits for them, and re-layouts: 4.83 us -> 3.19 us
    unnamed x14 -> x6, local copies, waits for them, and re-layouts: 4.32 us -> 2.68 us
where the time goes in v2:
time: 47.9 us; the launch traced here: 47.7 us
  Pallas kernels  43.9 us (92%)
  local copies, waits for them, and re-layouts  3.19 us (7%)
  between operations  0.65 us (1%)
    pallas_call x1, Pallas kernels, on_device(): pl.pallas_call(functools.partial(kernel, R, F, own), out_shape=(jax.Shape...  43.9 us
    unnamed x6, local copies, waits for them, and re-layouts  2.68 us

profile of v2, /device:TPU:1, one launch (start us, length us, event | category | flops | bytes accessed | tf_op | source)
XLA Modules:
  0.0 47.7 jit_solution(6600079583894715429)
XLA Ops:
  0.6 43.9 %shard_map.85 = (f32[4,16,256]{2,1,0:T(8,128)}, f32[1,128]{1,0:T(1,128)}, s32[16,128]{1,0:T(8,128)}) custom-call(s32[16]{0:T(128)} %sf_ref.1, s32[16]{0:T(128)} %sb_ref.1, s32[64,2048]{1,0:T(8,128)} %bins_ref.1, bf16[16,128]{1,0:T(8,128)(2,1)} %bitcast.10, bf16[16,128]{1,0:T(8,128)(2,1)} %bitcast.11, s32[16,128]{1,0:T(8,128)} %bitcast.7, s32[1,2048]{1,0:T(1,128)} %bitcast.8), custom_call_target="tpu_custom_call" | custom-call | tf_op jit(solution)/shard_map/pallas_call | solution.py:319
  44.5 0.0 copy-start.1
  44.5 0.6 %copy-done.1 = f32[1,128]{1,0:T(1,128)S(1)} copy-done((f32[1,128]{1,0:T(1,128)S(1)}, f32[1,128]{1,0:T(1,128)}, u32[]{:S(2)}) %copy-start.1) | copy-done | bytes 536
  45.1 0.5 %slice_bitcast_fusion = f32[16]{0:T(128)} fusion(f32[1,128]{1,0:T(1,128)S(1)} %copy-done.1), kind=kLoop, calls=%fused_computation | loop fusion | bytes 128 | tf_op jit(solution)/shard_map/squeeze | solution.py:358
  45.6 0.0 copy-start
  45.6 1.5 %copy.11 = f32[4,16,256]{2,1,0:T(8,128)} copy(f32[4,16,256]{2,1,0:T(8,128)} %get-tuple-element.12) | data formatting | bytes 131072
  47.1 0.0 copy-done
  47.1 0.6 %copy.12 = s32[2048]{0:T(1024)} copy(s32[2048]{0:T(1024)S(1)} %bitcast.9) | data formatting | bytes 16384
Async XLA Ops:
  44.5 0.6 %copy-start.1 = (f32[1,128]{1,0:T(1,128)S(1)}, f32[1,128]{1,0:T(1,128)}, u32[]{:S(2)}) copy-start(f32[1,128]{1,0:T(1,128)} %get-tuple-element.7) | copy-start | bytes 1540
  45.6 1.5 %copy-start = (s32[16,128]{1,0:T(8,128)S(1)}, s32[16,128]{1,0:T(8,128)}, u32[]{:S(2)}) copy-start(s32[16,128]{1,0:T(8,128)} %get-tuple-element.8) | copy-start | bytes 24580

commit v3 on v2

--- a/solution.py
+++ b/solution.py
@@ -29,7 +29,7 @@
            gain_ref, best_ref, child_ref,
            bins_v, picked, node_v, node_row_v, send, recv, weights, acc, right, rights, top, tops, high, highs,
            in_sem, send_sem, recv_sem, wsend_sem, wrecv_sem, fsend_sem, frecv_sem,
-           rsend_sem, rrecv_sem, tsend_sem, trecv_sem, hsend_sem, hrecv_sem):
+           rsend_sem, rrecv_sem, tsend_sem, trecv_sem, hsend_sem, hrecv_sem, column_in, all_in):
     feat_local, row_count = bins_v.shape
     tiles = row_count // LANES
     Z = R // 2
@@ -48,19 +48,39 @@
     for load in loads:
         load.start()
 
+    Y = min(8, F)
+    X = F // Y
+    me_x, me_y = me_f // Y, lax.rem(me_f, Y)
+
+    def feat_of(k):
+        return lax.rem(me_x + k // Y, X) * Y + lax.rem(me_y + lax.rem(k, Y), Y)
+
+    def hops(k):
+        x, y = k // Y, k % Y
+        return min(x, X - x) + min(y, Y - y)
+
+    far_feats = sorted(range(1, F), key=lambda k: -hops(k))
+    far_rows = sorted(range(1, R), key=lambda k: abs(k - R // 2))
+
     barrier = pltpu.get_barrier_semaphore()
 
     def greet_rows(k, c):
         pl.semaphore_signal(barrier, inc=1, device_id=(lax.rem(me_r + k, R), me_f), device_id_type=MESH)
         return c
 
-    def greet_feats(k, c):
-        pl.semaphore_signal(barrier, inc=1, device_id=(me_r, lax.rem(me_f + k, F)), device_id_type=MESH)
-        return c
-
-    lax.fori_loop(F // 2, F, greet_feats, 0)
-    lax.fori_loop(1, F // 2, greet_feats, 0)
-    lax.fori_loop(1, R, greet_rows, 0)
+    def over_feats(sem):
+        def greet(k, c):
+            pl.semaphore_signal(sem, inc=1, device_id=(me_r, feat_of(k)), device_id_type=MESH)
+            return c
+
+        lax.fori_loop(1, F, greet, 0)
+
+    lax.fori_loop(R // 2, R, greet_rows, 0)
+    lax.fori_loop(1, R // 2, greet_rows, 0)
+
+    @pl.when(me_z == 0)
+    def _():
+        over_feats(barrier)
 
     for load in loads:
         load.wait()
@@ -70,7 +90,11 @@
         send[j] = as_bf16(jnp.concatenate([block[:, t * LANES:(t + 1) * LANES] for t in range(tiles)], axis=0))
     recv[0, 0] = send[me_r]
 
-    pl.semaphore_wait(barrier, R + F - 2)
+    pl.semaphore_wait(barrier, jnp.where(me_z == 0, R + F - 2, R - 1))
+
+    @pl.when(me_z == 0)
+    def _():
+        over_feats(column_in)
 
     def bins_copy(d, o):
         to = 2 * lax.rem(me_z + d, Z) + (core if o == 0 else 1 - core)
@@ -81,45 +105,36 @@
 
     def bins_copy_to(d, o, to):
         return pltpu.make_async_remote_copy(
-            src_ref=send.at[to], dst_ref=recv.at[d, o], send_sem=send_sem.at[d, o], recv_sem=recv_sem.at[d, o],
+            src_ref=send.at[to], dst_ref=recv.at[d, o], send_sem=send_sem, recv_sem=recv_sem.at[d, o],
             device_id=(to, me_f), device_id_type=MESH)
 
     def weights_copy(d):
         return pltpu.make_async_remote_copy(
-            src_ref=weights.at[0, 0], dst_ref=weights.at[d, 0], send_sem=wsend_sem.at[d], recv_sem=wrecv_sem.at[d],
+            src_ref=weights.at[0, 0], dst_ref=weights.at[d, 0], send_sem=wsend_sem, recv_sem=wrecv_sem.at[d],
             device_id=(2 * lax.rem(me_z + d, Z) + core, me_f), device_id_type=MESH)
 
     def forward_copy(d):
         return pltpu.make_async_remote_copy(
-            src_ref=weights.at[d, 0], dst_ref=weights.at[d, 1], send_sem=fsend_sem.at[d], recv_sem=frecv_sem.at[d],
+            src_ref=weights.at[d, 0], dst_ref=weights.at[d, 1], send_sem=fsend_sem, recv_sem=frecv_sem.at[d],
             device_id=(2 * me_z + 1 - core, me_f), device_id_type=MESH)
 
     def right_copy(k):
         return pltpu.make_async_remote_copy(
-            src_ref=right, dst_ref=rights.at[k], send_sem=rsend_sem.at[k], recv_sem=rrecv_sem.at[k],
-            device_id=(me_r, lax.rem(me_f + k, F)), device_id_type=MESH)
+            src_ref=right, dst_ref=rights.at[k], send_sem=rsend_sem, recv_sem=rrecv_sem,
+            device_id=(me_r, feat_of(k)), device_id_type=MESH)
 
     def top_copy(k):
         return pltpu.make_async_remote_copy(
-            src_ref=top, dst_ref=tops.at[k], send_sem=tsend_sem.at[k], recv_sem=trecv_sem.at[k],
+            src_ref=top, dst_ref=tops.at[k], send_sem=tsend_sem, recv_sem=trecv_sem,
             device_id=(lax.rem(me_r + k, R), me_f), device_id_type=MESH)
 
     def high_copy(k):
         return pltpu.make_async_remote_copy(
-            src_ref=high, dst_ref=highs.at[k], send_sem=hsend_sem.at[k], recv_sem=hrecv_sem.at[k],
-            device_id=(me_r, lax.rem(me_f + k, F)), device_id_type=MESH)
-
-    def start(copy, k, c):
-        copy(k).start()
-        return c
-
-    def wait_recv(copy, k, c):
-        copy(k).wait_recv()
-        return c
-
-    def wait_send(copy, k, c):
-        copy(k).wait_send()
-        return c
+            src_ref=high, dst_ref=highs.at[k], send_sem=hsend_sem, recv_sem=hrecv_sem,
+            device_id=(me_r, feat_of(k)), device_id_type=MESH)
+
+    def wait_bytes(ref, sem):
+        pltpu.make_async_copy(ref, ref, sem).wait()
 
     def distance(i):
         odd = lax.rem(i, 2)
@@ -210,6 +225,16 @@
             @pl.when((lax.rem(k, 2) == 0) & (k // 2 + FIRST + 1 < Z))
             def _():
                 send_round(k // 2 + FIRST + 1)
+
+            @pl.when((me_z == 0) & (k == R // 2))
+            def _():
+                pl.semaphore_wait(column_in, F - 1)
+
+                def tell(z, c):
+                    pl.semaphore_signal(all_in, inc=1, device_id=(2 * z + core, me_f), device_id_type=MESH)
+                    return c
+
+                lax.fori_loop(1, Z, tell, 0)
 
             for t in range(blocks_of_chunk - 2):
                 stream(accs, chunk, t)
@@ -258,7 +283,8 @@
     diagonal = index == lax.broadcasted_iota(jnp.int32, (NODES, LANES), 1)
     top[...] = jnp.max(jnp.where(diagonal, best, -jnp.inf), axis=0, keepdims=True)
     tops[0] = top[...]
-    lax.fori_loop(1, R, lambda k, c: start(top_copy, k, c), 0)
+    for k in far_rows:
+        top_copy(k).start()
 
     first = me_f * feat_local
     split = jnp.zeros((NODES, LANES), jnp.int32)
@@ -277,35 +303,35 @@
         goes = jnp.where(jnp.broadcast_to(node_row[:, lanes], (NODES, LANES)) == index, goes, 0)
         parts.append(jnp.sum(goes.astype(jnp.float32), axis=0, keepdims=True))
     right[...] = jnp.concatenate(parts, axis=0).astype(BF16)
-    lax.fori_loop(1, F, lambda k, c: start(right_copy, k, c), 0)
-
-    lax.fori_loop(1, R, lambda k, c: wait_recv(top_copy, k, c), 0)
+    rights[0] = right[...]
+
+    @pl.when(me_z > 0)
+    def _():
+        pl.semaphore_wait(all_in, 1)
+
+    for k in far_feats:
+        right_copy(k).start()
+
+    wait_bytes(tops.at[pl.ds(1, R - 1)], trecv_sem)
     high[...] = jnp.max(tops[...], axis=0)
     highs[0] = high[...]
-    lax.fori_loop(1, F, lambda k, c: start(high_copy, k, c), 0)
-
-    rights[0] = right[...]
-    lax.fori_loop(1, F, lambda k, c: wait_recv(right_copy, k, c), 0)
+    for k in far_feats:
+        high_copy(k).start()
+
+    wait_bytes(rights.at[pl.ds(1, F - 1)], rrecv_sem)
     goes_right = jnp.zeros((tiles, LANES), jnp.float32)
     for k in range(F):
         goes_right = goes_right + rights[k].astype(jnp.float32)
     child_ref[...] = 2 * node_v[...] + goes_right.astype(jnp.int32)
 
-    def sent(d, c):
-        weights_copy(d).wait_send()
-        bins_copy(d, 0).wait_send()
-        bins_copy(d, 1).wait_send()
-        forward_copy(d).wait_send()
-        return c
-
-    forward_copy(0).wait_send()
-    bins_copy(0, 1).wait_send()
-    lax.fori_loop(1, Z, sent, 0)
-    lax.fori_loop(1, F, lambda k, c: wait_send(right_copy, k, c), 0)
-    lax.fori_loop(1, R, lambda k, c: wait_send(top_copy, k, c), 0)
-    lax.fori_loop(1, F, lambda k, c: wait_recv(high_copy, k, c), 0)
+    wait_bytes(send.at[pl.ds(0, R - 1)], send_sem)
+    wait_bytes(weights.at[pl.ds(1, Z - 1), 0], wsend_sem)
+    wait_bytes(weights.at[pl.ds(0, Z), 0], fsend_sem)
+    wait_bytes(rights.at[pl.ds(1, F - 1)], rsend_sem)
+    wait_bytes(tops.at[pl.ds(1, R - 1)], tsend_sem)
+    wait_bytes(highs.at[pl.ds(1, F - 1)], hrecv_sem)
     best_ref[...] = jnp.max(highs[...], axis=0)
-    lax.fori_loop(1, F, lambda k, c: wait_send(high_copy, k, c), 0)
+    wait_bytes(highs.at[pl.ds(1, F - 1)], hsend_sem)
 
 
 def on_device(R, F, bin_index, gradient, hessian, node_id, split_feature, split_bin):
@@ -341,12 +367,14 @@
             pltpu.VMEM((1, LANES), jnp.float32),
             pltpu.VMEM((F, 1, LANES), jnp.float32),
             dma((5,)),
-            dma((R // 2, 2)), dma((R // 2, 2)),
-            dma((R // 2,)), dma((R // 2,)),
-            dma((R // 2,)), dma((R // 2,)),
-            dma((F,)), dma((F,)),
-            dma((R,)), dma((R,)),
-            dma((F,)), dma((F,)),
+            dma(()), dma((R // 2, 2)),
+            dma(()), dma((R // 2,)),
+            dma(()), dma((R // 2,)),
+            dma(()), dma(()),
+            dma(()), dma(()),
+            dma(()), dma(()),
+            pltpu.SemaphoreType.REGULAR,
+            pltpu.SemaphoreType.REGULAR,
         ],
         compiler_params=pltpu.CompilerParams(
             collective_id=0, has_side_effects=True, vmem_limit_bytes=60 << 20),

time: 47.9 us -> 44.8 us (0.935)
  Pallas kernels: 43.9 us -> 40.7 us
    pallas_call x1, Pallas kernels: 43.9 us -> 40.7 us  [on_device(): pl.pallas_call(functools.partial(kernel, R, F, own), out_shape=(jax.Shape...]
where the time goes in v3:
time: 44.8 us; the launch traced here: 44.5 us
  Pallas kernels  40.7 us (91%)
  local copies, waits for them, and re-layouts  3.19 us (7%)
  between operations  0.65 us (1%)
    pallas_call x1, Pallas kernels, on_device(): pl.pallas_call(functools.partial(kernel, R, F, own), out_shape=(jax.Shape...  40.7 us
    unnamed x6, local copies, waits for them, and re-layouts  2.68 us

profile of v3, /device:TPU:1, one launch (start us, length us, event | category | flops | bytes accessed | tf_op | source)
XLA Modules:
  0.0 44.5 jit_solution(13812828398373992947)
XLA Ops:
  0.6 40.7 %shard_map.85 = (f32[4,16,256]{2,1,0:T(8,128)}, f32[1,128]{1,0:T(1,128)}, s32[16,128]{1,0:T(8,128)}) custom-call(s32[16]{0:T(128)} %sf_ref.1, s32[16]{0:T(128)} %sb_ref.1, s32[64,2048]{1,0:T(8,128)} %bins_ref.1, bf16[16,128]{1,0:T(8,128)(2,1)} %bitcast.10, bf16[16,128]{1,0:T(8,128)(2,1)} %bitcast.11, s32[16,128]{1,0:T(8,128)} %bitcast.7, s32[1,2048]{1,0:T(1,128)} %bitcast.8), custom_call_target="tpu_custom_call" | custom-call | tf_op jit(solution)/shard_map/pallas_call | solution.py:345
  41.3 0.0 copy-start.1
  41.4 0.6 %copy-done.1 = f32[1,128]{1,0:T(1,128)S(1)} copy-done((f32[1,128]{1,0:T(1,128)S(1)}, f32[1,128]{1,0:T(1,128)}, u32[]{:S(2)}) %copy-start.1) | copy-done | bytes 536
  41.9 0.5 %slice_bitcast_fusion = f32[16]{0:T(128)} fusion(f32[1,128]{1,0:T(1,128)S(1)} %copy-done.1), kind=kLoop, calls=%fused_computation | loop fusion | bytes 128 | tf_op jit(solution)/shard_map/squeeze | solution.py:386
  42.5 0.0 copy-start
  42.5 1.5 %copy.11 = f32[4,16,256]{2,1,0:T(8,128)} copy(f32[4,16,256]{2,1,0:T(8,128)} %get-tuple-element.12) | data formatting | bytes 131072
  43.9 0.0 copy-done
  43.9 0.6 %copy.12 = s32[2048]{0:T(1024)} copy(s32[2048]{0:T(1024)S(1)} %bitcast.9) | data formatting | bytes 16384
Async XLA Ops:
  41.3 0.6 %copy-start.1 = (f32[1,128]{1,0:T(1,128)S(1)}, f32[1,128]{1,0:T(1,128)}, u32[]{:S(2)}) copy-start(f32[1,128]{1,0:T(1,128)} %get-tuple-element.7) | copy-start | bytes 1540
  42.5 1.5 %copy-start = (s32[16,128]{1,0:T(8,128)S(1)}, s32[16,128]{1,0:T(8,128)}, u32[]{:S(2)}) copy-start(s32[16,128]{1,0:T(8,128)} %get-tuple-element.8) | copy-start | bytes 24580

commit v4 on v3

--- a/solution.py
+++ b/solution.py
@@ -25,9 +25,9 @@
     return x.astype(jnp.float32).astype(BF16)
 
 
-def kernel(R, F, own, sf_ref, sb_ref, bins_ref, grad_ref, hess_ref, node_ref, node_row_ref,
+def kernel(R, F, own, sf_in, sb_in, bins_ref, grad_ref, hess_ref, node_ref, node_row_ref,
            gain_ref, best_ref, child_ref,
-           bins_v, picked, node_v, node_row_v, send, recv, weights, acc, right, rights, top, tops, high, highs,
+           sf_ref, sb_ref, bins_v, picked, node_v, node_row_v, send, recv, weights, acc, right, rights, top, tops, high, highs,
            in_sem, send_sem, recv_sem, wsend_sem, wrecv_sem, fsend_sem, frecv_sem,
            rsend_sem, rrecv_sem, tsend_sem, trecv_sem, hsend_sem, hrecv_sem, column_in, all_in):
     feat_local, row_count = bins_v.shape
@@ -44,6 +44,8 @@
         pltpu.make_async_copy(hess_ref, weights.at[0, 0, tiles:2 * tiles, :], in_sem.at[2]),
         pltpu.make_async_copy(node_ref, node_v, in_sem.at[3]),
         pltpu.make_async_copy(node_row_ref, node_row_v, in_sem.at[4]),
+        pltpu.make_async_copy(sf_in, sf_ref, in_sem.at[5]),
+        pltpu.make_async_copy(sb_in, sb_ref, in_sem.at[6]),
     ]
     for load in loads:
         load.start()
@@ -334,12 +336,23 @@
     wait_bytes(highs.at[pl.ds(1, F - 1)], hsend_sem)
 
 
+def finish(gain_in, best_in, child_in, gain_ref, best_ref, child_ref, sem):
+    moves = [
+        pltpu.make_async_copy(gain_in, gain_ref, sem.at[0]),
+        pltpu.make_async_copy(child_in, child_ref, sem.at[1]),
+    ]
+    for move in moves:
+        move.start()
+    best_ref[...] = best_in[0, 0:NODES]
+    for move in moves:
+        move.wait()
+
+
 def on_device(R, F, bin_index, gradient, hessian, node_id, split_feature, split_bin):
     feat_local, row_count = bin_index.shape
     own = feat_local // R
     tiles = row_count // LANES
     vmem = pl.BlockSpec(memory_space=pltpu.VMEM)
-    smem = pl.BlockSpec(memory_space=pltpu.SMEM)
     hbm = pl.BlockSpec(memory_space=pltpu.HBM)
     dma = pltpu.SemaphoreType.DMA
     gain, best, child = pl.pallas_call(
@@ -349,9 +362,11 @@
             jax.ShapeDtypeStruct((1, LANES), jnp.float32),
             jax.ShapeDtypeStruct((tiles, LANES), jnp.int32),
         ),
-        in_specs=[smem, smem, hbm, hbm, hbm, hbm, hbm],
+        in_specs=[hbm] * 7,
         out_specs=(vmem, vmem, vmem),
         scratch_shapes=[
+            pltpu.SMEM((NODES,), jnp.int32),
+            pltpu.SMEM((NODES,), jnp.int32),
             pltpu.VMEM((feat_local, row_count), jnp.int32),
             pltpu.VMEM((NODES, row_count), jnp.int32),
             pltpu.VMEM((tiles, LANES), jnp.int32),
@@ -366,7 +381,7 @@
             pltpu.VMEM((R, 1, LANES), jnp.float32),
             pltpu.VMEM((1, LANES), jnp.float32),
             pltpu.VMEM((F, 1, LANES), jnp.float32),
-            dma((5,)),
+            dma((7,)),
             dma(()), dma((R // 2, 2)),
             dma(()), dma((R // 2,)),
             dma(()), dma((R // 2,)),
@@ -377,13 +392,26 @@
             pltpu.SemaphoreType.REGULAR,
         ],
         compiler_params=pltpu.CompilerParams(
-            collective_id=0, has_side_effects=True, vmem_limit_bytes=60 << 20),
+            collective_id=0, has_side_effects=True, vmem_limit_bytes=32 << 20),
     )(
-        split_feature, split_bin, bin_index,
-        gradient.reshape(tiles, LANES), hessian.reshape(tiles, LANES),
-        node_id.reshape(tiles, LANES), node_id.reshape(1, row_count),
+        *(pltpu.with_memory_space_constraint(x, pltpu.HBM) for x in (
+            split_feature, split_bin, bin_index,
+            gradient.reshape(tiles, LANES), hessian.reshape(tiles, LANES),
+            node_id.reshape(tiles, LANES), node_id.reshape(1, row_count)))
     )
-    return gain, best[0, :NODES], child.reshape(row_count)
+    gain, best, child = pl.pallas_call(
+        finish,
+        out_shape=(
+            jax.ShapeDtypeStruct(gain.shape, gain.dtype),
+            jax.ShapeDtypeStruct((NODES,), best.dtype),
+            jax.ShapeDtypeStruct(child.shape, child.dtype),
+        ),
+        in_specs=[vmem, vmem, vmem],
+        out_specs=(hbm, vmem, hbm),
+        scratch_shapes=[dma((2,))],
+        compiler_params=pltpu.CompilerParams(vmem_limit_bytes=32 << 20),
+    )(gain, best, child)
+    return gain, best, child.reshape(row_count)
 
 
 def solution(mesh):

time: 44.8 us -> 41.4 us (0.924)
  local copies, waits for them, and re-layouts: 3.19 us -> 0 us
    unnamed x6 -> x0, local copies, waits for them, and re-layouts: 2.68 us -> none
    pallas_call x1, Pallas kernels: 40.7 us -> 39.4 us  [on_device(): pl.pallas_call(functools.partial(kernel, R, F, own), out_shape=(jax.Shape...]
    pallas_call x0 -> x1, Pallas kernels: none -> 1.16 us  [on_device(): pl.pallas_call(finish, out_shape=(jax.ShapeDtypeStruct(gain.shape, gain.d...]
    squeeze x1 -> x0, local copies, waits for them, and re-layouts: 0.51 us -> none  [on_device(): return (gain, best[0, :NODES], child.reshape(row_count))]
where the time goes in v4:
time: 41.4 us; the launch traced here: 41.2 us
  Pallas kernels  40.6 us (98%)
  between operations  0.64 us (2%)
    pallas_call x1, Pallas kernels, on_device(): pl.pallas_call(functools.partial(kernel, R, F, own), out_shape=(jax.Shape...  39.4 us
    pallas_call x1, Pallas kernels, on_device(): pl.pallas_call(finish, out_shape=(jax.ShapeDtypeStruct(gain.shape, gain.d...  1.16 us

profile of v4, /device:TPU:1, one launch (start us, length us, event | category | flops | bytes accessed | tf_op | source)
XLA Modules:
  0.0 41.2 jit_solution(8459625724039813025)
XLA Ops:
  0.6 39.4 %shard_map.85 = (f32[4,16,256]{2,1,0:T(8,128)S(1)}, f32[1,128]{1,0:T(1,128)S(1)}, s32[16,128]{1,0:T(8,128)S(1)}) custom-call(s32[16]{0:T(128)} %sf_in.1, s32[16]{0:T(128)} %sb_in.1, s32[64,2048]{1,0:T(8,128)} %bins_ref.1, bf16[16,128]{1,0:T(8,128)(2,1)} %bitcast.7, bf16[16,128]{1,0:T(8,128)(2,1)} %bitcast.8, s32[16,128]{1,0:T(8,128)} %bitcast.5, ...), custom_call_target="tpu_custom_call" | custom-call | tf_op jit(solution)/shard_map/pallas_call | solution.py:358
  40.1 1.2 %shard_map.86 = (f32[4,16,256]{2,1,0:T(8,128)}, f32[16]{0:T(128)}, s32[16,128]{1,0:T(8,128)}) custom-call(f32[4,16,256]{2,1,0:T(8,128)S(1)} %get-tuple-element.9.gain_in, f32[1,128]{1,0:T(1,128)S(1)} %get-tuple-element.10.best_in, s32[16,128]{1,0:T(8,128)S(1)} %get-tuple-element.11.child_in), custom_call_target="tpu_custom_call" | custom-call | tf_op jit(solution)/shard_map/pallas_call | solution.py:402

commit v5 on v4

--- a/solution.py
+++ b/solution.py
@@ -14,7 +14,7 @@
 LANES = 128
 BF16 = jnp.bfloat16
 MESH = pl.DeviceIdType.MESH
-FIRST = 3
+FIRST = 4
 
 
 def sublane_index(rows, lanes):
@@ -29,7 +29,7 @@
            gain_ref, best_ref, child_ref,
            sf_ref, sb_ref, bins_v, picked, node_v, node_row_v, send, recv, weights, acc, right, rights, top, tops, high, highs,
            in_sem, send_sem, recv_sem, wsend_sem, wrecv_sem, fsend_sem, frecv_sem,
-           rsend_sem, rrecv_sem, tsend_sem, trecv_sem, hsend_sem, hrecv_sem, column_in, all_in):
+           rsend_sem, rrecv_sem, tsend_sem, trecv_sem, hsend_sem, hrecv_sem, ready, column_in, all_in):
     feat_local, row_count = bins_v.shape
     tiles = row_count // LANES
     Z = R // 2
@@ -47,9 +47,6 @@
         pltpu.make_async_copy(sf_in, sf_ref, in_sem.at[5]),
         pltpu.make_async_copy(sb_in, sb_ref, in_sem.at[6]),
     ]
-    for load in loads:
-        load.start()
-
     Y = min(8, F)
     X = F // Y
     me_x, me_y = me_f // Y, lax.rem(me_f, Y)
@@ -66,9 +63,12 @@
 
     barrier = pltpu.get_barrier_semaphore()
 
-    def greet_rows(k, c):
-        pl.semaphore_signal(barrier, inc=1, device_id=(lax.rem(me_r + k, R), me_f), device_id_type=MESH)
-        return c
+    def over_rows(sem, first, last):
+        def greet(r, c):
+            pl.semaphore_signal(sem, inc=1, device_id=(r, me_f), device_id_type=MESH)
+            return c
+
+        lax.fori_loop(first, last, greet, 0)
 
     def over_feats(sem):
         def greet(k, c):
@@ -77,12 +77,17 @@
 
         lax.fori_loop(1, F, greet, 0)
 
-    lax.fori_loop(R // 2, R, greet_rows, 0)
-    lax.fori_loop(1, R // 2, greet_rows, 0)
+    pl.semaphore_signal(barrier, inc=1, device_id=(2 * me_z + 1 - core, me_f), device_id_type=MESH)
+    over_rows(barrier, 2 * (me_z + 1), R)
 
     @pl.when(me_z == 0)
     def _():
         over_feats(barrier)
+
+    for load in loads:
+        load.start()
+    pl.semaphore_wait(barrier, jnp.where(me_z == 0, F, 2 * me_z + 1))
+    over_rows(ready.at[me_r], 0, 2 * me_z)
 
     for load in loads:
         load.wait()
@@ -92,12 +97,6 @@
         send[j] = as_bf16(jnp.concatenate([block[:, t * LANES:(t + 1) * LANES] for t in range(tiles)], axis=0))
     recv[0, 0] = send[me_r]
 
-    pl.semaphore_wait(barrier, jnp.where(me_z == 0, R + F - 2, R - 1))
-
-    @pl.when(me_z == 0)
-    def _():
-        over_feats(column_in)
-
     def bins_copy(d, o):
         to = 2 * lax.rem(me_z + d, Z) + (core if o == 0 else 1 - core)
         return bins_copy_to(d, o, to)
@@ -144,27 +143,36 @@
 
     forward_copy(0).start()
     bins_copy(0, 1).start()
-    weights_copy(distance(1)).start()
+    def send_weights(d):
+        @pl.when(me_z + d < Z)
+        def _():
+            for o in range(2):
+                pl.semaphore_wait(ready.at[2 * (me_z + d) + o], 1)
+
+        weights_copy(d).start()
 
     def send_round(i):
+        bins_copy(distance(i), 0).start()
+        bins_copy(distance(i), 1).start()
+
         @pl.when(i < Z - 1)
         def _():
-            weights_copy(distance(i + 1)).start()
-
-        bins_copy(distance(i), 0).start()
-        bins_copy(distance(i), 1).start()
+            send_weights(distance(i + 1))
+
+    send_weights(distance(1))
 
     def first_round(i, c):
         send_round(i)
         return c
 
-    lax.fori_loop(1, FIRST + 1, first_round, 0)
+    lax.fori_loop(1, min(FIRST, Z - 1) + 1, first_round, 0)
 
     span = 2
     depth = span * LANES
     blocks_of_chunk = tiles // span
     zero = jnp.zeros((NODES, depth), BF16)
     high_rows = 2 * NODES * HI
+    MET = max(2, Z - FIRST) + 1
 
     def over_lanes(ref, d, o, base, t, stride, rows):
         return jnp.concatenate(
@@ -224,11 +232,15 @@
             def _():
                 pass_on(distance(k // 2 + 1))
 
-            @pl.when((lax.rem(k, 2) == 0) & (k // 2 + FIRST + 1 < Z))
+            @pl.when((k >= 2) & (k - 1 + FIRST < Z))
             def _():
-                send_round(k // 2 + FIRST + 1)
-
-            @pl.when((me_z == 0) & (k == R // 2))
+                send_round(k - 1 + FIRST)
+
+            @pl.when((me_z == 0) & (k == MET))
+            def _():
+                over_feats(column_in)
+
+            @pl.when((me_z == 0) & (k == R - 3))
             def _():
                 pl.semaphore_wait(column_in, F - 1)
 
@@ -336,14 +348,16 @@
     wait_bytes(highs.at[pl.ds(1, F - 1)], hsend_sem)
 
 
-def finish(gain_in, best_in, child_in, gain_ref, best_ref, child_ref, sem):
+def finish(gain_in, best_in, child_in, gain_ref, best_ref, child_ref, best_v, sem):
     moves = [
         pltpu.make_async_copy(gain_in, gain_ref, sem.at[0]),
         pltpu.make_async_copy(child_in, child_ref, sem.at[1]),
+        pltpu.make_async_copy(best_v, best_ref, sem.at[2]),
     ]
-    for move in moves:
-        move.start()
-    best_ref[...] = best_in[0, 0:NODES]
+    moves[0].start()
+    moves[1].start()
+    best_v[...] = best_in[0, 0:NODES]
+    moves[2].start()
     for move in moves:
         move.wait()
 
@@ -388,6 +402,7 @@
             dma(()), dma(()),
             dma(()), dma(()),
             dma(()), dma(()),
+            pltpu.SemaphoreType.REGULAR((R,)),
             pltpu.SemaphoreType.REGULAR,
             pltpu.SemaphoreType.REGULAR,
         ],
@@ -407,8 +422,8 @@
             jax.ShapeDtypeStruct(child.shape, child.dtype),
         ),
         in_specs=[vmem, vmem, vmem],
-        out_specs=(hbm, vmem, hbm),
-        scratch_shapes=[dma((2,))],
+        out_specs=(hbm, hbm, hbm),
+        scratch_shapes=[pltpu.VMEM((NODES,), best.dtype), dma((3,))],
         compiler_params=pltpu.CompilerParams(vmem_limit_bytes=32 << 20),
     )(gain, best, child)
     return gain, best, child.reshape(row_count)

time: 41.4 us -> 40.6 us (0.981)
  Pallas kernels: 40.6 us -> 39.9 us
    pallas_call x1, Pallas kernels: 1.16 us -> 0.66 us  [on_device(): pl.pallas_call(finish, out_shape=(jax.ShapeDtypeStruct(gain.shape, gain.d...]
where the time goes in v5:
time: 40.6 us; the launch traced here: 40.5 us
  Pallas kernels  39.9 us (98%)
  between operations  0.64 us (2%)
    pallas_call x1, Pallas kernels, on_device(): pl.pallas_call(functools.partial(kernel, R, F, own), out_shape=(jax.Shape...  39.2 us

profile of v5, /device:TPU:1, one launch (start us, length us, event | category | flops | bytes accessed | tf_op | source)
XLA Modules:
  0.0 40.5 jit_solution(7937597880084764685)
XLA Ops:
  0.6 39.2 %shard_map.85 = (f32[4,16,256]{2,1,0:T(8,128)S(1)}, f32[1,128]{1,0:T(1,128)S(1)}, s32[16,128]{1,0:T(8,128)S(1)}) custom-call(s32[16]{0:T(128)} %sf_in.1, s32[16]{0:T(128)} %sb_in.1, s32[64,2048]{1,0:T(8,128)} %bins_ref.1, bf16[16,128]{1,0:T(8,128)(2,1)} %bitcast.7, bf16[16,128]{1,0:T(8,128)(2,1)} %bitcast.8, s32[16,128]{1,0:T(8,128)} %bitcast.5, ...), custom_call_target="tpu_custom_call" | custom-call | tf_op jit(solution)/shard_map/pallas_call | solution.py:372
  39.8 0.7 %shard_map.86 = (f32[4,16,256]{2,1,0:T(8,128)}, f32[16]{0:T(128)}, s32[16,128]{1,0:T(8,128)}) custom-call(f32[4,16,256]{2,1,0:T(8,128)S(1)} %get-tuple-element.9.gain_in, f32[1,128]{1,0:T(1,128)S(1)} %get-tuple-element.10.best_in, s32[16,128]{1,0:T(8,128)S(1)} %get-tuple-element.11.child_in), custom_call_target="tpu_custom_call" | custom-call | tf_op jit(solution)/shard_map/pallas_call | solution.py:417

commit v6 on v5

--- a/solution.py
+++ b/solution.py
@@ -172,7 +172,7 @@
     blocks_of_chunk = tiles // span
     zero = jnp.zeros((NODES, depth), BF16)
     high_rows = 2 * NODES * HI
-    MET = max(2, Z - FIRST) + 1
+    MET = max(3, Z - FIRST + 1) + 1
 
     def over_lanes(ref, d, o, base, t, stride, rows):
         return jnp.concatenate(
@@ -232,9 +232,9 @@
             def _():
                 pass_on(distance(k // 2 + 1))
 
-            @pl.when((k >= 2) & (k - 1 + FIRST < Z))
+            @pl.when((k >= 3) & (k - 2 + FIRST < Z))
             def _():
-                send_round(k - 1 + FIRST)
+                send_round(k - 2 + FIRST)
 
             @pl.when((me_z == 0) & (k == MET))
             def _():
@@ -275,14 +275,14 @@
             pltpu.ACC(0)((own * high_rows, own * LO), jnp.float32),
             pltpu.ACC(1)((own * high_rows, own * LO), jnp.float32))
 
-    best = jnp.full((NODES, 1), -jnp.inf, jnp.float32)
+    highest = jnp.full((NODES, BINS), -jnp.inf, jnp.float32)
     for f in range(own):
+        parts = [acc[f, level * 2 * NODES:(level + 1) * 2 * NODES, :] for level in range(HI)]
+        carry = jnp.zeros((2 * NODES, 1), jnp.float32)
         blocks = []
-        carry = jnp.zeros((2 * NODES, 1), jnp.float32)
-        for level in range(HI):
-            block = acc[f, level * 2 * NODES:(level + 1) * 2 * NODES, :] + carry
-            carry = block[:, LO - 1:LO]
-            blocks.append(block)
+        for part in parts:
+            blocks.append(part + carry)
+            carry = part[:, LO - 1:LO] + carry
         left = jnp.concatenate(blocks, axis=1)
         left_grad, left_hess = left[:NODES], left[NODES:]
         total_grad, total_hess = carry[:NODES], carry[NODES:]
@@ -291,7 +291,8 @@
                 + right_grad * right_grad / (total_hess - left_hess + 1.0)
                 - total_grad * total_grad / (total_hess + 1.0))
         gain_ref[f] = gain
-        best = jnp.maximum(best, jnp.max(gain, axis=1, keepdims=True))
+        highest = jnp.maximum(highest, gain)
+    best = jnp.max(highest, axis=1, keepdims=True)
 
     index = sublane_index(NODES, LANES)
     diagonal = index == lax.broadcasted_iota(jnp.int32, (NODES, LANES), 1)

time: 40.6 us -> 40.5 us (level)
  no operation moved by 1% of the time
where the time goes in v6:
time: 40.5 us; the launch traced here: 40.4 us
  Pallas kernels  39.8 us (98%)
  between operations  0.64 us (2%)
    pallas_call x1, Pallas kernels, on_device(): pl.pallas_call(functools.partial(kernel, R, F, own), out_shape=(jax.Shape...  39.1 us

profile of v6, /device:TPU:1, one launch (start us, length us, event | category | flops | bytes accessed | tf_op | source)
XLA Modules:
  0.0 40.4 jit_solution(9539224326861287598)
XLA Ops:
  0.6 39.1 %shard_map.85 = (f32[4,16,256]{2,1,0:T(8,128)S(1)}, f32[1,128]{1,0:T(1,128)S(1)}, s32[16,128]{1,0:T(8,128)S(1)}) custom-call(s32[16]{0:T(128)} %sf_in.1, s32[16]{0:T(128)} %sb_in.1, s32[64,2048]{1,0:T(8,128)} %bins_ref.1, bf16[16,128]{1,0:T(8,128)(2,1)} %bitcast.7, bf16[16,128]{1,0:T(8,128)(2,1)} %bitcast.8, s32[16,128]{1,0:T(8,128)} %bitcast.5, ...), custom_call_target="tpu_custom_call" | custom-call | tf_op jit(solution)/shard_map/pallas_call | solution.py:373
  39.7 0.7 %shard_map.86 = (f32[4,16,256]{2,1,0:T(8,128)}, f32[16]{0:T(128)}, s32[16,128]{1,0:T(8,128)}) custom-call(f32[4,16,256]{2,1,0:T(8,128)S(1)} %get-tuple-element.9.gain_in, f32[1,128]{1,0:T(1,128)S(1)} %get-tuple-element.10.best_in, s32[16,128]{1,0:T(8,128)S(1)} %get-tuple-element.11.child_in), custom_call_target="tpu_custom_call" | custom-call | tf_op jit(solution)/shard_map/pallas_call | solution.py:418

commit v7 on v6

--- a/solution.py
+++ b/solution.py
@@ -87,7 +87,9 @@
     for load in loads:
         load.start()
     pl.semaphore_wait(barrier, jnp.where(me_z == 0, F, 2 * me_z + 1))
-    over_rows(ready.at[me_r], 0, 2 * me_z)
+    farthest = 2 * jnp.maximum(me_z - Z // 2, 0)
+    over_rows(ready.at[me_r], farthest, 2 * me_z)
+    over_rows(ready.at[me_r], 0, farthest)
 
     for load in loads:
         load.wait()

time: 40.5 us -> 40.5 us (level)
  no operation moved by 1% of the time
where the time goes in v7:
time: 40.5 us; the launch traced here: 40.4 us
  Pallas kernels  39.8 us (98%)
  between operations  0.64 us (2%)
    pallas_call x1, Pallas kernels, on_device(): pl.pallas_call(functools.partial(kernel, R, F, own), out_shape=(jax.Shape...  39.1 us

profile of v7, /device:TPU:1, one launch (start us, length us, event | category | flops | bytes accessed | tf_op | source)
XLA Modules:
  0.0 40.4 jit_solution(7739609478191407642)
XLA Ops:
  0.6 39.1 %shard_map.85 = (f32[4,16,256]{2,1,0:T(8,128)S(1)}, f32[1,128]{1,0:T(1,128)S(1)}, s32[16,128]{1,0:T(8,128)S(1)}) custom-call(s32[16]{0:T(128)} %sf_in.1, s32[16]{0:T(128)} %sb_in.1, s32[64,2048]{1,0:T(8,128)} %bins_ref.1, bf16[16,128]{1,0:T(8,128)(2,1)} %bitcast.7, bf16[16,128]{1,0:T(8,128)(2,1)} %bitcast.8, s32[16,128]{1,0:T(8,128)} %bitcast.5, ...), custom_call_target="tpu_custom_call" | custom-call | tf_op jit(solution)/shard_map/pallas_call | solution.py:375
  39.8 0.7 %shard_map.86 = (f32[4,16,256]{2,1,0:T(8,128)}, f32[16]{0:T(128)}, s32[16,128]{1,0:T(8,128)}) custom-call(f32[4,16,256]{2,1,0:T(8,128)S(1)} %get-tuple-element.9.gain_in, f32[1,128]{1,0:T(1,128)S(1)} %get-tuple-element.10.best_in, s32[16,128]{1,0:T(8,128)S(1)} %get-tuple-element.11.child_in), custom_call_target="tpu_custom_call" | custom-call | tf_op jit(solution)/shard_map/pallas_call | solution.py:420
